TPU v7x, 32 devices: a whole 2x2x4 slice. The times are simulated.
32 devices in a mesh: section: 4 (over x, core), ep: 8 (over z, y).
Axes of the slice: x: 2, y: 2, z: 4, core: 2. Of those that a mesh axis runs over, the one named last changes fastest.
Arguments:
- states: bfloat16 [4, 1024, 6144], P('section', 'ep'), may hold values from -6 to 6
- expert_ids: int32 [4, 1024, 2], P('section', 'ep'), may hold values from 0 to 7, all different within a row; in each aligned block of 128 rows (0 to 127, 128 to 255, ..., all dimensions but the last counted through in order) at most 48 rows name the same one
- gate_values: float32 [4, 1024, 2], P('section', 'ep'), may hold values from 0.1 to 1
- keep_mask: int32 [4, 1024, 2], P('section', 'ep'), may hold values 0 or 1
- w_gate: bfloat16 [4, 6144, 16384], P('section', None, 'ep'), may hold values from -0.078125 to 0.078125
- w_up: bfloat16 [4, 6144, 16384], P('section', None, 'ep'), may hold values from -0.078125 to 0.078125
- w_down: bfloat16 [4, 16384, 6144], P('section', 'ep'), may hold values from -0.0625 to 0.0625
Outputs:
- next_states: bfloat16 [4, 1024, 6144], P('section', 'ep')
Inputs may be any that keep to these rules, and one draw needn't show every extreme that they name: `expert_ids`: in every section and every aligned block of 128 tokens (the rows of one index of ep), no expert is named by more than 48 tokens, a bound that some block reaches; the 2 experts of a token differ.
All inputs are finite; a program needn't handle non-finite values. No bound on the sum of `keep_mask` on one device may be relied on, other than what follows from the above.
Results may differ from a plain program's by a relative error of at most 0.0057.
Values may be sent and summed in bfloat16 or wider, within the bound.
A program may use at most 128 MiB of HBM per device.

v0:
```python
import jax
import jax.numpy as jnp
from jax import lax
from jax.sharding import PartitionSpec as P

EXP_WIN = 2
CAP = 48


def from_behind(value, axis, by):
    devices = lax.axis_size(axis)
    return lax.ppermute(value, axis, [(i, (i + by) % devices) for i in range(devices)])


def expert_mlp(row_block, gate_matrix, up_matrix, down_matrix):
    count_a, count_b, row_width = row_block.shape
    flat_rows = row_block.reshape(count_a * count_b, row_width)
    gate_proj = jnp.dot(flat_rows, gate_matrix, preferred_element_type=jnp.float32)
    up_proj = jnp.dot(flat_rows, up_matrix, preferred_element_type=jnp.float32)
    hidden = (jax.nn.silu(gate_proj) * up_proj).astype(jnp.bfloat16)
    partial_out = jnp.dot(hidden, down_matrix, preferred_element_type=jnp.float32).astype(
        jnp.bfloat16
    )
    return partial_out.reshape(count_a, count_b, row_width)


def send_back(partial_out):
    return lax.all_to_all(partial_out, "ep", split_axis=0, concat_axis=0, tiled=True)


def dispatch_rows(outgoing, worker):
    return worker(lax.all_to_all(outgoing, "ep", split_axis=0, concat_axis=0, tiled=True))


def body(states, expert_ids, gate_values, keep_mask, w_gate, w_up, w_down):
    tokens_here = states[0]
    ids_here = expert_ids[0]
    gates_here = gate_values[0]
    keep_here = keep_mask[0]
    gate_matrix = w_gate[0]
    up_matrix = w_up[0]
    down_matrix = w_down[0]
    slices = lax.axis_size("ep") // EXP_WIN
    model_width = tokens_here.shape[1]
    expert_range = jnp.arange(EXP_WIN, dtype=jnp.int32)
    chosen = ((ids_here[None] == expert_range[:, None, None]) & (keep_here[None] == 1)).astype(
        jnp.int32
    )
    picked = jnp.sum(chosen, axis=2)
    weights_tok = jnp.sum(chosen.astype(jnp.float32) * gates_here[None], axis=2)
    slot_index = jnp.cumsum(picked, axis=1) - 1
    positions = jnp.arange(CAP, dtype=jnp.int32)
    dispatch_table = (
        (slot_index[:, None, :] == positions[None, :, None]) & (picked[:, None, :] == 1)
    ).astype(jnp.float32)
    compact = jnp.einsum(
        "ect,td->ecd",
        dispatch_table.astype(jnp.bfloat16),
        tokens_here,
        preferred_element_type=jnp.float32,
    ).astype(jnp.bfloat16)

    def local_expert(row_block):
        return expert_mlp(row_block, gate_matrix, up_matrix, down_matrix)

    outgoing = jnp.repeat(compact, slices, axis=0)
    partials = dispatch_rows(outgoing, local_expert)
    returned = send_back(partials)
    expert_out = jnp.sum(
        returned.reshape(EXP_WIN, slices, CAP, model_width).astype(jnp.float32), axis=1
    )
    combine = dispatch_table * weights_tok[:, None, :]
    mixed = jnp.einsum("ect,ecd->td", combine, expert_out, precision=lax.Precision.HIGHEST).astype(
        jnp.bfloat16
    )
    return from_behind(mixed[None], "section", 1)


def solution(mesh):
    return jax.shard_map(
        body,
        mesh=mesh,
        in_specs=(
            P("section", "ep", None),
            P("section", "ep", None),
            P("section", "ep", None),
            P("section", "ep", None),
            P("section", None, "ep"),
            P("section", None, "ep"),
            P("section", "ep", None),
        ),
        out_specs=P("section", "ep", None),
        check_vma=False,
    )
```

profile of v0, /device:TPU:0, one launch (start us, length us, event | category | flops | bytes accessed | tf_op | source)
XLA Modules:
  0.0 294.5 jit_solution(2195989759637409143)
XLA Ops:
  0.0 0.0 copy-start
  0.0 0.8 compare_bitcast_fusion
  0.8 0.7 fusion.26
  1.5 0.3 reduce_window_sum.11
  1.8 0.0 copy-done
  1.8 0.5 convolution_convert_fusion
  2.3 0.5 broadcast_in_dim.4
  2.9 111.5 %all_to_all.10 = bf16[8,48,6144]{2,1,0:T(8,128)(2,1)S(1)} all-to-all(bf16[8,48,6144]{2,1,0:T(8,128)(2,1)S(1)} %bitcast.48), channel_id=1, replica_groups=mesh['section'=4,'ep'=8] {'ep'}, dimensions={0} | all-to-all | bytes 9437184 | tf_op jit(solution)/shard_map/all_to_all | solution.py:32
  114.4 13.6 %fusion.4 = f32[384,2048]{1,0:T(8,128)S(1)} fusion(bf16[384,6144]{1,0:T(8,128)(2,1)S(1)} %bitcast.50, bf16[1,6144,2048]{2,1,0:T(8,128)(2,1)} %param.11), kind=kOutput, calls=%fused_computation.4 | convolution fusion | flops 9663676416 | bytes 33030144 | tf_op jit(solution)/shard_map/dot_general | solution.py:18
  127.9 14.9 %multiply_convert_fusion.clone.4 = bf16[384,2048]{1,0:T(8,128)(2,1)S(1)} fusion(f32[384,2048]{1,0:T(8,128)S(1)} %fusion.4, bf16[384,6144]{1,0:T(8,128)(2,1)S(1)} %bitcast.51, bf16[1,6144,2048]{2,1,0:T(8,128)(2,1)} %param.12), kind=kOutput, calls=%fused_computation.12.clone.clone.clone.1 | convolution fusion | flops 9668395008 | bytes 34603008 | tf_op jit(solution)/shard_map/dot_general | solution.py:19
  142.8 16.1 %fusion.6 = bf16[384,6144]{1,0:T(8,128)(2,1)} fusion(bf16[1,2048,6144]{2,1,0:T(8,128)(2,1)} %param.13, bf16[384,2048]{1,0:T(8,128)(2,1)S(1)} %multiply_convert_fusion.clone.4), kind=kOutput, calls=%fused_computation.7 | convolution fusion | flops 9666035712 | bytes 31457280 | tf_op jit(solution)/shard_map/dot_general | solution.py:21
  158.9 0.0 copy-start.2
  159.0 0.0 copy-start.3
  159.0 4.9 %all-to-all-start.1 = ((bf16[8,48,6144]{2,1,0:T(8,128)(2,1)}), bf16[8,48,6144]{2,1,0:T(8,128)(2,1)}, u32[]{:S(2)}, u32[]{:S(2)}) async-start(bf16[8,48,6144]{2,1,0:T(8,128)(2,1)} %bitcast.49), calls=%async_computation.1 | async-start | bytes 9437184 | tf_op jit(solution)/shard_map/all_to_all | solution.py:28
  163.9 0.0 copy-done.2
  163.9 0.0 copy-done.3
  163.9 103.3 %all-to-all-done.1 = bf16[8,48,6144]{2,1,0:T(8,128)(2,1)} async-done(((bf16[8,48,6144]{2,1,0:T(8,128)(2,1)}), bf16[8,48,6144]{2,1,0:T(8,128)(2,1)}, u32[]{:S(2)}, u32[]{:S(2)}) %all-to-all-start.1) | async-done | bytes 4718624 | tf_op jit(solution)/shard_map/all_to_all | solution.py:28
  267.2 0.0 copy-start.1
  267.2 3.5 %convert_reduce_fusion = f32[2,48,6144]{2,1,0:T(8,128)S(1)} fusion(bf16[8,48,6144]{2,1,0:T(8,128)(2,1)} %all-to-all-done.1), kind=kLoop, calls=%fused_computation.6 | loop fusion | flops 4128768 | bytes 7077888 | tf_op jit(solution)/shard_map/reduce_sum | solution.py:69
  270.7 2.7 fusion.10
  273.4 0.1 collective-permute-start
  273.5 19.8 %collective-permute-done = bf16[1,128,6144]{2,1,0:T(8,128)(2,1)S(1)} collective-permute-done((bf16[1,128,6144]{2,1,0:T(8,128)(2,1)S(1)}, bf16[1,128,6144]{2,1,0:T(8,128)(2,1)S(1)}, u32[]{:S(2)}, u32[]{:S(2)}) %collective-permute-start) | collective-permute-done | bytes 1572896 | tf_op jit(solution)/shard_map/ppermute | solution.py:12
  293.3 1.1 copy.12
  294.5 0.0 copy-done.1
  (3 shorter events, 0.0 us)
Async XLA Ops:
  0.0 1.8 copy-start
  158.9 4.9 %copy-start.2 = (s32[1,128,2]{1,2,0:T(2,128)S(1)}, s32[1,128,2]{1,2,0:T(2,128)}, u32[]{:S(2)}) copy-start(s32[1,128,2]{1,2,0:T(2,128)} %param.8) | copy-start | bytes 3076
  159.0 4.9 %copy-start.3 = (f32[1,128,2]{1,2,0:T(2,128)S(1)}, f32[1,128,2]{1,2,0:T(2,128)}, u32[]{:S(2)}) copy-start(f32[1,128,2]{1,2,0:T(2,128)} %param.9) | copy-start | bytes 3076
  159.0 108.3 %all-to-all-start.1 = ((bf16[8,48,6144]{2,1,0:T(8,128)(2,1)}), bf16[8,48,6144]{2,1,0:T(8,128)(2,1)}, u32[]{:S(2)}, u32[]{:S(2)}) async-start(bf16[8,48,6144]{2,1,0:T(8,128)(2,1)} %bitcast.49), calls=%async_computation.1 | async-start | bytes 9437184 | tf_op jit(solution)/shard_map/all_to_all | solution.py:28
  267.2 27.2 %copy-start.1 = (bf16[1,128,6144]{2,1,0:T(8,128)(2,1)S(1)}, bf16[1,128,6144]{2,1,0:T(8,128)(2,1)}, u32[]{:S(2)}) copy-start(bf16[1,128,6144]{2,1,0:T(8,128)(2,1)} %param.7) | copy-start | bytes 4718596
  273.4 19.9 %collective-permute-start = (bf16[1,128,6144]{2,1,0:T(8,128)(2,1)S(1)}, bf16[1,128,6144]{2,1,0:T(8,128)(2,1)S(1)}, u32[]{:S(2)}, u32[]{:S(2)}) collective-permute-start(bf16[1,128,6144]{2,1,0:T(8,128)(2,1)S(1)} %fusion.10), channel_id=1, source_target_pairs={{0,8},{8,16},{16,24},{24,0},{1,9},{9,17},{17,25},{25,1},{2,10},{10... | collective-permute-start | bytes 4718600 | tf_op jit(solution)/shard_map/ppermute | solution.py:12
where the time goes:
time: 295 us; the launch traced here: 294 us
  waiting for transfers between devices  123 us (42%)
  blocking collectives  111 us (38%)
  matrix products  47.7 us (16%)
  other arithmetic  5.32 us (2%)
  starting transfers between devices  4.96 us (2%)
    all_to_all x1, blocking collectives, dispatch_rows(): lax.all_to_all(outgoing, 'ep', split_axis=0, concat_axis=0, tiled=True)  111 us
    all_to_all x1, waiting for transfers between devices, send_back(): lax.all_to_all(partial_out, 'ep', split_axis=0, concat_axis=0, tiled=True)  103 us
    ppermute x1, waiting for transfers between devices, from_behind(): lax.ppermute(value, axis, [(i, (i + by) % devices) for i in range(devices)])  19.8 us
    dot_general x1, matrix products, expert_mlp(): jnp.dot(hidden, down_matrix, preferred_element_type=jnp.float32)  16.1 us
    dot_general x1, matrix products, expert_mlp(): up_proj = jnp.dot(flat_rows, up_matrix, preferred_element_type=jnp.float32)  14.9 us
    dot_general x1, matrix products, expert_mlp(): jnp.dot(flat_rows, gate_matrix, preferred_element_type=jnp.float32)  13.6 us
  transfers between devices with their start and end apart: 2, of which 2 were waited for; matrix products, arithmetic and copies ran while one was open for 0% of the time, Pallas kernels for 0%

commit v1 on v0

v1 whole, which is shorter than its diff:
```python
import functools

import jax
import jax.numpy as jnp
from jax import lax
from jax.experimental import pallas as pl
from jax.experimental.pallas import tpu as pltpu
from jax.sharding import PartitionSpec as P

EXP_WIN = 2
CAP = 48
CHUNK = 512
RING = 3
GROUP = 4
MESH = pl.DeviceIdType.MESH

A_ME, B_ME, A_Y, B_Y, A_Z, B_Z, A_Q, B_Q = range(8)

(
    X_CROSS, X_AY, X_AZ, X_BY, X_BZ, X_FA, X_FB,
    R_BQ, R_AQ, R_BY, R_AZ, R_SY, R_SZ, R_CROSS, R_OUT,
) = range(15)
KINDS = 15


def moe_kernel(
    chunks, width,
    tab_ref, spread_ref, wcol_ref, states_ref, wg_ref, wu_ref, wd_ref,
    out_ref,
    rows, other, wg_buf, wu_buf, wd_buf, gate, up, hidden, part,
    sum_y, sum_z, sum_b, sum_a, mixed, landed,
    send_sem, recv_sem, wg_sem, wu_sem, wd_sem,
):
    section = lax.axis_index("section")
    ep = lax.axis_index("ep")
    sections = lax.axis_size("section")
    dev_y = (section, ep + 1 - 2 * (ep % 2))
    dev_z = (section, ep + 2 - 4 * ((ep // 2) % 2))
    dev_x = (section, (ep + 4) % 8)
    dev_next = ((section + 1) % sections, ep)
    dev_prev = ((section + sections - 1) % sections, ep)
    units = hidden.shape[1]

    def block(slot):
        return pl.ds(slot * CAP, CAP)

    def copy(kind, k):
        def row(slot):
            return rows.at[k, block(slot)]

        def piece(slot):
            return part.at[k, block(slot)]

        columns = pl.ds(pl.multiple_of(k * width, width), width)
        src, dst, dev = {
            X_CROSS: lambda: (other.at[k], row(B_ME), dev_x),
            X_AY: lambda: (row(A_ME), row(A_Y), dev_y),
            X_AZ: lambda: (row(A_ME), row(A_Z), dev_z),
            X_BY: lambda: (row(B_ME), row(B_Y), dev_y),
            X_BZ: lambda: (row(B_ME), row(B_Z), dev_z),
            X_FA: lambda: (row(A_Y), row(A_Q), dev_z),
            X_FB: lambda: (row(B_Z), row(B_Q), dev_y),
            R_BQ: lambda: (piece(B_Q), landed.at[0, k], dev_y),
            R_AQ: lambda: (piece(A_Q), landed.at[1, k], dev_z),
            R_BY: lambda: (piece(B_Y), landed.at[2, k], dev_y),
            R_AZ: lambda: (piece(A_Z), landed.at[3, k], dev_z),
            R_SY: lambda: (sum_y.at[k], landed.at[4, k], dev_y),
            R_SZ: lambda: (sum_z.at[k], landed.at[5, k], dev_z),
            R_CROSS: lambda: (sum_b.at[k], landed.at[6, k], dev_x),
            R_OUT: lambda: (mixed.at[k], out_ref.at[0, :, columns], dev_next),
        }[kind]()
        return pltpu.make_async_remote_copy(
            src_ref=src,
            dst_ref=dst,
            send_sem=send_sem.at[kind, k],
            recv_sem=recv_sem.at[kind, k],
            device_id=dev,
            device_id_type=MESH,
        )

    def in_weights(k):
        slot = k % RING
        depth = pl.ds(pl.multiple_of(k * width, width), width)
        return (
            pltpu.make_async_copy(wg_ref.at[0, depth], wg_buf.at[slot], wg_sem.at[slot]),
            pltpu.make_async_copy(wu_ref.at[0, depth], wu_buf.at[slot], wu_sem.at[slot]),
        )

    def out_weights(k):
        slot = k % RING
        columns = pl.ds(pl.multiple_of(k * width, width), width)
        return pltpu.make_async_copy(
            wd_ref.at[0, :, columns], wd_buf.at[slot], wd_sem.at[slot]
        )

    for k in range(RING):
        for c in in_weights(k):
            c.start()

    barrier = pltpu.get_barrier_semaphore()
    for dev in (dev_y, dev_z, dev_x, dev_next, dev_prev):
        pl.semaphore_signal(barrier, inc=1, device_id=dev, device_id_type=MESH)

    for k in range(chunks):
        picked = jnp.dot(
            tab_ref[...],
            states_ref[0, :, k * width:(k + 1) * width],
            preferred_element_type=jnp.float32,
        ).astype(jnp.bfloat16)
        rows[k, block(A_ME)] = picked[:CAP]
        other[k] = picked[CAP:]

    pl.semaphore_wait(barrier, 5)

    for k in range(RING):
        out_weights(k).start()

    gate[...] = jnp.zeros_like(gate)
    up[...] = jnp.zeros_like(up)
    tile = min(units, 512)

    def in_step(i, carry):
        @pl.when(i < chunks)
        def _():
            for kind in (X_CROSS, X_AY, X_AZ):
                copy(kind, i).start()

        @pl.when((i >= 2) & (i < chunks + 2))
        def _():
            k = i - 2
            copy(X_CROSS, k).wait_recv()
            copy(X_BZ, k).start()
            copy(X_BY, k).start()
            copy(X_AY, k).wait_recv()
            copy(X_FA, k).start()

        @pl.when((i >= 3) & (i < chunks + 3))
        def _():
            k = i - 3
            copy(X_BZ, k).wait_recv()
            copy(X_FB, k).start()

        @pl.when(i >= 4)
        def _():
            k = i - 4
            for kind in (X_AZ, X_BY, X_FA, X_FB):
                copy(kind, k).wait_recv()
            for c in in_weights(k):
                c.wait()
            slot = k % RING
            for n in range(0, units, tile):
                gate[:, n:n + tile] += jnp.dot(
                    rows[k], wg_buf[slot, :, n:n + tile], preferred_element_type=jnp.float32
                )
                up[:, n:n + tile] += jnp.dot(
                    rows[k], wu_buf[slot, :, n:n + tile], preferred_element_type=jnp.float32
                )

            @pl.when(k + RING < chunks)
            def _():
                for c in in_weights(k + RING):
                    c.start()

        return carry

    lax.fori_loop(0, chunks + 4, in_step, 0)

    def act_step(r, carry):
        at = pl.ds(pl.multiple_of(r * 16, 16), 16)
        g = gate[at]
        hidden[at] = ((g / (1.0 + jnp.exp(-g))) * up[at]).astype(jnp.bfloat16)
        return carry

    lax.fori_loop(0, hidden.shape[0] // 16, act_step, 0)

    def wide(value):
        return value.astype(jnp.float32)

    def out_step(i, carry):
        @pl.when(i < chunks)
        def _():
            out_weights(i).wait()
            part[i] = jnp.dot(
                hidden[...], wd_buf[i % RING], preferred_element_type=jnp.float32
            ).astype(jnp.bfloat16)
            for kind in (R_BQ, R_AQ, R_BY, R_AZ):
                copy(kind, i).start()

            @pl.when(i + RING < chunks)
            def _():
                out_weights(i + RING).start()

            for kind in range(X_CROSS, X_FB + 1):
                copy(kind, i).wait_send()

        @pl.when((i >= 1) & (i < chunks + 1))
        def _():
            k = i - 1
            copy(R_AQ, k).wait_recv()
            sum_y[k] = (wide(part[k, block(A_Y)]) + wide(landed[1, k])).astype(jnp.bfloat16)
            copy(R_SY, k).start()
            copy(R_BQ, k).wait_recv()
            sum_z[k] = (wide(part[k, block(B_Z)]) + wide(landed[0, k])).astype(jnp.bfloat16)
            copy(R_SZ, k).start()

        @pl.when((i >= 2) & (i < chunks + 2))
        def _():
            k = i - 2
            copy(R_BY, k).wait_recv()
            copy(R_SZ, k).wait_recv()
            sum_b[k] = (
                wide(part[k, block(B_ME)]) + wide(landed[2, k]) + wide(landed[5, k])
            ).astype(jnp.bfloat16)
            copy(R_CROSS, k).start()
            copy(R_AZ, k).wait_recv()
            copy(R_SY, k).wait_recv()
            sum_a[k] = wide(part[k, block(A_ME)]) + wide(landed[3, k]) + wide(landed[4, k])

        @pl.when(i >= 4)
        def _():
            k = i - 4
            copy(R_CROSS, k).wait_recv()
            scaled = jnp.concatenate([sum_a[k], wide(landed[6, k])], axis=0) * wcol_ref[...]
            high = scaled.astype(jnp.bfloat16)
            low = (scaled - wide(high)).astype(jnp.bfloat16)
            mixed[k] = jnp.dot(
                spread_ref[...],
                jnp.concatenate([high, low], axis=0),
                preferred_element_type=jnp.float32,
            ).astype(jnp.bfloat16)
            copy(R_OUT, k).start()
            for kind in range(R_BQ, R_CROSS + 1):
                copy(kind, k).wait_send()

        return carry

    lax.fori_loop(0, chunks + 4, out_step, 0)

    def last_step(k, carry):
        copy(R_OUT, k).wait_send()
        copy(R_OUT, k).wait_recv()
        return carry

    lax.fori_loop(0, chunks, last_step, 0)


def moe_call(tab, spread, wcol, states, w_gate, w_up, w_down):
    tokens, model = states.shape[1:]
    units = w_gate.shape[2]
    width = min(CHUNK, model // RING)
    chunks = model // width
    total = 2 * GROUP * CAP
    bf16, f32 = jnp.bfloat16, jnp.float32
    vmem = pl.BlockSpec(memory_space=pltpu.VMEM)
    hbm = pl.BlockSpec(memory_space=pl.ANY)
    return pl.pallas_call(
        functools.partial(moe_kernel, chunks, width),
        out_shape=jax.ShapeDtypeStruct((1, tokens, model), bf16),
        in_specs=[vmem, vmem, vmem, vmem, hbm, hbm, hbm],
        out_specs=hbm,
        scratch_shapes=[
            pltpu.VMEM((chunks, total, width), bf16),
            pltpu.VMEM((chunks, CAP, width), bf16),
            pltpu.VMEM((RING, width, units), bf16),
            pltpu.VMEM((RING, width, units), bf16),
            pltpu.VMEM((RING, units, width), bf16),
            pltpu.VMEM((total, units), f32),
            pltpu.VMEM((total, units), f32),
            pltpu.VMEM((total, units), bf16),
            pltpu.VMEM((chunks, total, width), bf16),
            pltpu.VMEM((chunks, CAP, width), bf16),
            pltpu.VMEM((chunks, CAP, width), bf16),
            pltpu.VMEM((chunks, CAP, width), bf16),
            pltpu.VMEM((chunks, CAP, width), f32),
            pltpu.VMEM((chunks, tokens, width), bf16),
            pltpu.VMEM((7, chunks, CAP, width), bf16),
            pltpu.SemaphoreType.DMA((KINDS, chunks)),
            pltpu.SemaphoreType.DMA((KINDS, chunks)),
            pltpu.SemaphoreType.DMA((RING,)),
            pltpu.SemaphoreType.DMA((RING,)),
            pltpu.SemaphoreType.DMA((RING,)),
        ],
        cost_estimate=pl.CostEstimate(
            flops=6 * total * model * units,
            bytes_accessed=6 * model * units,
            transcendentals=total * units,
        ),
        compiler_params=pltpu.CompilerParams(
            collective_id=0, has_side_effects=True, vmem_limit_bytes=60 * 1024 * 1024
        ),
    )(tab, spread, wcol, states, w_gate, w_up, w_down)


def routing(ids_here, gates_here, keep_here, order):
    chosen = (ids_here[None] == order[:, None, None]) & (keep_here[None] == 1)
    picked = jnp.any(chosen, axis=2)
    weights_tok = jnp.sum(jnp.where(chosen, gates_here[None], 0.0), axis=2)
    slot_index = jnp.cumsum(picked.astype(jnp.int32), axis=1) - 1
    positions = jnp.arange(CAP, dtype=jnp.int32)
    table = (slot_index[:, None, :] == positions[None, :, None]) & picked[:, None, :]
    return table, weights_tok


def grouped_body(states, expert_ids, gate_values, keep_mask, w_gate, w_up, w_down):
    mine = lax.axis_index("ep") // GROUP
    order = jnp.stack([mine, 1 - mine]).astype(jnp.int32)
    table, weights_tok = routing(expert_ids[0], gate_values[0], keep_mask[0], order)
    wcol = jnp.sum(jnp.where(table, weights_tok[:, None, :], 0.0), axis=2)
    tab = table.reshape(EXP_WIN * CAP, -1).astype(jnp.bfloat16)
    spread = jnp.concatenate([tab.T, tab.T], axis=1)
    return moe_call(
        tab, spread, wcol.reshape(EXP_WIN * CAP, 1), states, w_gate, w_up, w_down
    )


def general_body(states, expert_ids, gate_values, keep_mask, w_gate, w_up, w_down):
    slices = lax.axis_size("ep") // EXP_WIN
    order = jnp.arange(EXP_WIN, dtype=jnp.int32)
    table, weights_tok = routing(expert_ids[0], gate_values[0], keep_mask[0], order)
    compact = jnp.einsum(
        "ect,td->ecd",
        table.astype(jnp.bfloat16),
        states[0],
        preferred_element_type=jnp.float32,
    ).astype(jnp.bfloat16)
    arrived = lax.all_to_all(
        jnp.repeat(compact, slices, axis=0), "ep", split_axis=0, concat_axis=0, tiled=True
    )
    flat = arrived.reshape(-1, arrived.shape[2])
    gate = jnp.dot(flat, w_gate[0], preferred_element_type=jnp.float32)
    up = jnp.dot(flat, w_up[0], preferred_element_type=jnp.float32)
    hidden = (jax.nn.silu(gate) * up).astype(jnp.bfloat16)
    piece = jnp.dot(hidden, w_down[0], preferred_element_type=jnp.float32).astype(jnp.bfloat16)
    returned = lax.all_to_all(
        piece.reshape(arrived.shape), "ep", split_axis=0, concat_axis=0, tiled=True
    )
    expert_out = jnp.sum(
        returned.reshape(EXP_WIN, slices, CAP, -1).astype(jnp.float32), axis=1
    )
    combine = table.astype(jnp.float32) * weights_tok[:, None, :]
    mixed = jnp.einsum("ect,ecd->td", combine, expert_out, precision=lax.Precision.HIGHEST)
    sections = lax.axis_size("section")
    return lax.ppermute(
        mixed.astype(jnp.bfloat16)[None],
        "section",
        [(i, (i + 1) % sections) for i in range(sections)],
    )


def solution(mesh):
    grouped = mesh.shape["ep"] == EXP_WIN * GROUP and mesh.shape["section"] > 2
    return jax.shard_map(
        grouped_body if grouped else general_body,
        mesh=mesh,
        in_specs=(
            P("section", "ep", None),
            P("section", "ep", None),
            P("section", "ep", None),
            P("section", "ep", None),
            P("section", None, "ep"),
            P("section", None, "ep"),
            P("section", "ep", None),
        ),
        out_specs=P("section", "ep", None),
        check_vma=False,
    )
```

time: 295 us -> 134 us (0.45)
  Pallas kernels: 0 us -> 126 us
  waiting for transfers between devices: 123 us -> 0 us
  blocking collectives: 111 us -> 0 us
  matrix products: 47.7 us -> 0 us
  starting transfers between devices: 4.96 us -> 0 us
    pallas_call x0 -> x1, Pallas kernels: none -> 126 us  [moe_call(): pl.pallas_call(functools.partial(moe_kernel, chunks, width), out_shape=ja...]
    all_to_all x1 -> x0, blocking collectives: 111 us -> none  [dispatch_rows(): lax.all_to_all(outgoing, 'ep', split_axis=0, concat_axis=0, tiled=True)]
    all_to_all x1 -> x0, waiting for transfers between devices: 103 us -> none  [send_back(): lax.all_to_all(partial_out, 'ep', split_axis=0, concat_axis=0, tiled=True)]
    dot_general x5 -> x0, matrix products: 47.7 us -> none  [the longest x1 16.1 us: expert_mlp(): jnp.dot(hidden, down_matrix, preferred_element_type=jnp.float32)]
    ppermute x1 -> x0, waiting for transfers between devices: 19.8 us -> none  [from_behind(): lax.ppermute(value, axis, [(i, (i + by) % devices) for i in range(devices)])]
    all_to_all x1 -> x0, starting transfers between devices: 4.9 us -> none  [send_back(): lax.all_to_all(partial_out, 'ep', split_axis=0, concat_axis=0, tiled=True)]
    reduce_sum x3 -> x2, other arithmetic: 4.2 us -> 0.88 us  [the longest x1 0.78 us: routing(): weights_tok = jnp.sum(jnp.where(chosen, gates_here[None], 0.0), axis=2)]
  transfers between devices with their start and end apart: 2 -> 0, of which waited for: 2 -> 0; matrix products, arithmetic and copies ran while one was open for 0% -> 0% of each run, Pallas kernels for 0% -> 0%
where the time goes in v1:
time: 134 us
  Pallas kernels  126 us (94%)
  local copies, waits for them, and re-layouts  4.44 us (3%)
  other arithmetic  3.46 us (3%)
    pallas_call x1, Pallas kernels, moe_call(): pl.pallas_call(functools.partial(moe_kernel, chunks, width), out_shape=ja...  126 us
    unnamed x1, local copies, waits for them, and re-layouts  2.69 us

profile of v1, /device:TPU:0, one launch (start us, length us, event | category | flops | bytes accessed | tf_op | source)
XLA Modules:
  0.0 134.1 jit_solution(4265741111175652385)
XLA Ops:
  0.0 0.1 pad_add_fusion
  0.1 0.7 compare_bitcast_fusion
  0.8 0.8 fusion.2
  1.5 0.8 fusion.3
  2.3 0.3 reduce_window_sum.11
  2.6 0.1 select_reduce_fusion
  2.7 0.1 eq.54
  2.8 0.1 copy.28
  3.0 0.1 copy.26
  3.1 0.7 copy.29.tab_ref
  3.8 0.7 reshape.20.wcol_ref
  4.5 0.7 pad_maximum_fusion.spread_ref
  5.3 126.1 %shard_map.73 = bf16[1,128,6144]{2,1,0:T(8,128)(2,1)} custom-call(bf16[96,128]{1,0:T(8,128)(2,1)} %copy.29.tab_ref, bf16[128,192]{1,0:T(8,128)(2,1)} %pad_maximum_fusion.spread_ref, f32[96,1]{1,0:T(8,128)} %reshape.20.wcol_ref, bf16[1,128,6144]{2,1,0:T(8,128)(2,1)} %states_ref.1, bf16[1,6144,2048]{2,1,0:T(8,128)(2,1)} %wg_ref.1, ...), custom_call_target="tpu_custom_call" | custom-call | flops 28991029248 | bytes 75497472 | tf_op jit(solution)/shard_map/pallas_call | solution.py:256
  131.4 2.7 %copy.32 = bf16[1,128,6144]{2,1,0:T(8,128)(2,1)} copy(bf16[1,128,6144]{2,1,0:T(8,128)(2,1)} %shard_map.73) | data formatting | bytes 3145728
  (6 shorter events, 0.0 us)

commit v2 on v1

--- a/solution.py
+++ b/solution.py
@@ -11,6 +11,7 @@
 CAP = 48
 CHUNK = 512
 RING = 3
+LANES = 128
 GROUP = 4
 MESH = pl.DeviceIdType.MESH
 
@@ -25,8 +26,9 @@
 
 def moe_kernel(
     chunks, width,
-    tab_ref, spread_ref, wcol_ref, states_ref, wg_ref, wu_ref, wd_ref,
+    ids_ref, gates_ref, keep_ref, states_ref, wg_ref, wu_ref, wd_ref,
     out_ref,
+    tab, spread, wcol,
     rows, other, wg_buf, wu_buf, wd_buf, gate, up, hidden, part,
     sum_y, sum_z, sum_b, sum_a, mixed, landed,
     send_sem, recv_sem, wg_sem, wu_sem, wd_sem,
@@ -34,15 +36,29 @@
     section = lax.axis_index("section")
     ep = lax.axis_index("ep")
     sections = lax.axis_size("section")
-    dev_y = (section, ep + 1 - 2 * (ep % 2))
-    dev_z = (section, ep + 2 - 4 * ((ep // 2) % 2))
+    ep_y = ep + 1 - 2 * (ep % 2)
+    ep_z = ep + 2 - 4 * ((ep // 2) % 2)
+    dev_y = (section, ep_y)
+    dev_z = (section, ep_z)
     dev_x = (section, (ep + 4) % 8)
     dev_next = ((section + 1) % sections, ep)
     dev_prev = ((section + sections - 1) % sections, ep)
     units = hidden.shape[1]
 
     def block(slot):
-        return pl.ds(slot * CAP, CAP)
+        return pl.ds(pl.multiple_of(slot * CAP, 16), CAP)
+
+    def z_then_y(k):
+        return (section, ep_z + (k % 2) * (ep_y - ep_z))
+
+    def y_then_z(k):
+        return (section, ep_y + (k % 2) * (ep_z - ep_y))
+
+    def y_then_z_slot(k):
+        return A_Y + (k % 2) * (A_Z - A_Y)
+
+    def z_then_y_slot(k):
+        return A_Z + (k % 2) * (A_Y - A_Z)
 
     def copy(kind, k):
         def row(slot):
@@ -58,13 +74,13 @@
             X_AZ: lambda: (row(A_ME), row(A_Z), dev_z),
             X_BY: lambda: (row(B_ME), row(B_Y), dev_y),
             X_BZ: lambda: (row(B_ME), row(B_Z), dev_z),
-            X_FA: lambda: (row(A_Y), row(A_Q), dev_z),
+            X_FA: lambda: (row(y_then_z_slot(k)), row(A_Q), z_then_y(k)),
             X_FB: lambda: (row(B_Z), row(B_Q), dev_y),
             R_BQ: lambda: (piece(B_Q), landed.at[0, k], dev_y),
-            R_AQ: lambda: (piece(A_Q), landed.at[1, k], dev_z),
+            R_AQ: lambda: (piece(A_Q), landed.at[1, k], z_then_y(k)),
             R_BY: lambda: (piece(B_Y), landed.at[2, k], dev_y),
-            R_AZ: lambda: (piece(A_Z), landed.at[3, k], dev_z),
-            R_SY: lambda: (sum_y.at[k], landed.at[4, k], dev_y),
+            R_AZ: lambda: (piece(z_then_y_slot(k)), landed.at[3, k], z_then_y(k)),
+            R_SY: lambda: (sum_y.at[k], landed.at[4, k], y_then_z(k)),
             R_SZ: lambda: (sum_z.at[k], landed.at[5, k], dev_z),
             R_CROSS: lambda: (sum_b.at[k], landed.at[6, k], dev_x),
             R_OUT: lambda: (mixed.at[k], out_ref.at[0, :, columns], dev_next),
@@ -101,14 +117,47 @@
     for dev in (dev_y, dev_z, dev_x, dev_next, dev_prev):
         pl.semaphore_signal(barrier, inc=1, device_id=dev, device_id_type=MESH)
 
-    for k in range(chunks):
-        picked = jnp.dot(
-            tab_ref[...],
-            states_ref[0, :, k * width:(k + 1) * width],
-            preferred_element_type=jnp.float32,
+    tokens = states_ref.shape[1]
+    mine = ep // GROUP
+
+    def choice(expert):
+        chosen = (ids_ref[0] == expert) & (keep_ref[0] == 1)
+        picked = jnp.sum(jnp.where(chosen, 1.0, 0.0), axis=0, keepdims=True)
+        weight = jnp.sum(jnp.where(chosen, gates_ref[0], 0.0), axis=0, keepdims=True)
+        return picked, weight
+
+    picked_own, weight_own = choice(mine)
+    picked_other, weight_other = choice(1 - mine)
+    before = lax.broadcasted_iota(jnp.int32, (tokens, tokens), 0)
+    token = lax.broadcasted_iota(jnp.int32, (tokens, tokens), 1)
+    slot_row = lax.broadcasted_iota(jnp.int32, (LANES, tokens), 0)
+    own = slot_row < CAP
+    picked = jnp.where(own, picked_own, jnp.where(slot_row < 2 * CAP, picked_other, 0.0))
+    rank = jnp.dot(
+        picked.astype(jnp.bfloat16),
+        jnp.where(before <= token, 1.0, 0.0).astype(jnp.bfloat16),
+        preferred_element_type=jnp.float32,
+    )
+    place = jnp.where(own, slot_row, slot_row - CAP).astype(jnp.float32)
+    table = jnp.where((picked > 0.5) & (rank - 1.0 == place), 1.0, 0.0)
+    tab[...] = table.astype(jnp.bfloat16)
+    wcol[...] = jnp.sum(
+        table * jnp.where(own, weight_own, weight_other), axis=1, keepdims=True
+    )
+    across = jnp.transpose(table).astype(jnp.bfloat16)
+    spread[:, :LANES] = across
+    spread[:, LANES:] = across
+
+    def gather(k):
+        columns = pl.ds(pl.multiple_of(k * width, width), width)
+        taken = jnp.dot(
+            tab[: 2 * CAP], states_ref[0, :, columns], preferred_element_type=jnp.float32
         ).astype(jnp.bfloat16)
-        rows[k, block(A_ME)] = picked[:CAP]
-        other[k] = picked[CAP:]
+        rows[k, block(A_ME)] = taken[:CAP]
+        other[k] = taken[CAP:]
+
+    for k in range(2):
+        gather(k)
 
     pl.semaphore_wait(barrier, 5)
 
@@ -119,11 +168,21 @@
     up[...] = jnp.zeros_like(up)
     tile = min(units, 512)
 
+    def arrived(k):
+        for kind in (X_BY, X_FA, X_FB):
+            copy(kind, k).wait_recv()
+        for c in in_weights(k):
+            c.wait()
+
     def in_step(i, carry):
         @pl.when(i < chunks)
         def _():
             for kind in (X_CROSS, X_AY, X_AZ):
                 copy(kind, i).start()
+
+        @pl.when(i + 2 < chunks)
+        def _():
+            gather(i + 2)
 
         @pl.when((i >= 2) & (i < chunks + 2))
         def _():
@@ -132,6 +191,7 @@
             copy(X_BZ, k).start()
             copy(X_BY, k).start()
             copy(X_AY, k).wait_recv()
+            copy(X_AZ, k).wait_recv()
             copy(X_FA, k).start()
 
         @pl.when((i >= 3) & (i < chunks + 3))
@@ -143,10 +203,7 @@
         @pl.when(i >= 4)
         def _():
             k = i - 4
-            for kind in (X_AZ, X_BY, X_FA, X_FB):
-                copy(kind, k).wait_recv()
-            for c in in_weights(k):
-                c.wait()
+            arrived(k)
             slot = k % RING
             for n in range(0, units, tile):
                 gate[:, n:n + tile] += jnp.dot(
@@ -163,15 +220,20 @@
 
         return carry
 
-    lax.fori_loop(0, chunks + 4, in_step, 0)
-
-    def act_step(r, carry):
-        at = pl.ds(pl.multiple_of(r * 16, 16), 16)
-        g = gate[at]
-        hidden[at] = ((g / (1.0 + jnp.exp(-g))) * up[at]).astype(jnp.bfloat16)
-        return carry
-
-    lax.fori_loop(0, hidden.shape[0] // 16, act_step, 0)
+    lax.fori_loop(0, chunks + 3, in_step, 0)
+
+    last = chunks - 1
+    arrived(last)
+    tile = min(units, 256)
+    for n in range(0, units, tile):
+        at = slice(n, n + tile)
+        g = gate[:, at] + jnp.dot(
+            rows[last], wg_buf[last % RING, :, at], preferred_element_type=jnp.float32
+        )
+        u = up[:, at] + jnp.dot(
+            rows[last], wu_buf[last % RING, :, at], preferred_element_type=jnp.float32
+        )
+        hidden[:, at] = ((g / (1.0 + jnp.exp(-g))) * u).astype(jnp.bfloat16)
 
     def wide(value):
         return value.astype(jnp.float32)
@@ -197,7 +259,7 @@
         def _():
             k = i - 1
             copy(R_AQ, k).wait_recv()
-            sum_y[k] = (wide(part[k, block(A_Y)]) + wide(landed[1, k])).astype(jnp.bfloat16)
+            sum_y[k] = (wide(part[k, block(y_then_z_slot(k))]) + wide(landed[1, k])).astype(jnp.bfloat16)
             copy(R_SY, k).start()
             copy(R_BQ, k).wait_recv()
             sum_z[k] = (wide(part[k, block(B_Z)]) + wide(landed[0, k])).astype(jnp.bfloat16)
@@ -220,11 +282,13 @@
         def _():
             k = i - 4
             copy(R_CROSS, k).wait_recv()
-            scaled = jnp.concatenate([sum_a[k], wide(landed[6, k])], axis=0) * wcol_ref[...]
+            unused = jnp.zeros((LANES - 2 * CAP, width), jnp.float32)
+            values = jnp.concatenate([sum_a[k], wide(landed[6, k]), unused], axis=0)
+            scaled = values * wcol[...]
             high = scaled.astype(jnp.bfloat16)
             low = (scaled - wide(high)).astype(jnp.bfloat16)
             mixed[k] = jnp.dot(
-                spread_ref[...],
+                spread[...],
                 jnp.concatenate([high, low], axis=0),
                 preferred_element_type=jnp.float32,
             ).astype(jnp.bfloat16)
@@ -244,7 +308,7 @@
     lax.fori_loop(0, chunks, last_step, 0)
 
 
-def moe_call(tab, spread, wcol, states, w_gate, w_up, w_down):
+def moe_call(expert_ids, gate_values, keep_mask, states, w_gate, w_up, w_down):
     tokens, model = states.shape[1:]
     units = w_gate.shape[2]
     width = min(CHUNK, model // RING)
@@ -259,6 +323,9 @@
         in_specs=[vmem, vmem, vmem, vmem, hbm, hbm, hbm],
         out_specs=hbm,
         scratch_shapes=[
+            pltpu.VMEM((LANES, tokens), bf16),
+            pltpu.VMEM((tokens, 2 * LANES), bf16),
+            pltpu.VMEM((LANES, 1), f32),
             pltpu.VMEM((chunks, total, width), bf16),
             pltpu.VMEM((chunks, CAP, width), bf16),
             pltpu.VMEM((RING, width, units), bf16),
@@ -288,7 +355,7 @@
         compiler_params=pltpu.CompilerParams(
             collective_id=0, has_side_effects=True, vmem_limit_bytes=60 * 1024 * 1024
         ),
-    )(tab, spread, wcol, states, w_gate, w_up, w_down)
+    )(expert_ids, gate_values, keep_mask, states, w_gate, w_up, w_down)
 
 
 def routing(ids_here, gates_here, keep_here, order):
@@ -302,15 +369,10 @@
 
 
 def grouped_body(states, expert_ids, gate_values, keep_mask, w_gate, w_up, w_down):
-    mine = lax.axis_index("ep") // GROUP
-    order = jnp.stack([mine, 1 - mine]).astype(jnp.int32)
-    table, weights_tok = routing(expert_ids[0], gate_values[0], keep_mask[0], order)
-    wcol = jnp.sum(jnp.where(table, weights_tok[:, None, :], 0.0), axis=2)
-    tab = table.reshape(EXP_WIN * CAP, -1).astype(jnp.bfloat16)
-    spread = jnp.concatenate([tab.T, tab.T], axis=1)
-    return moe_call(
-        tab, spread, wcol.reshape(EXP_WIN * CAP, 1), states, w_gate, w_up, w_down
-    )
+    expert_ids, gate_values, keep_mask = (
+        jnp.swapaxes(value, 1, 2) for value in (expert_ids, gate_values, keep_mask)
+    )
+    return moe_call(expert_ids, gate_values, keep_mask, states, w_gate, w_up, w_down)
 
 
 def general_body(states, expert_ids, gate_values, keep_mask, w_gate, w_up, w_down):

time: 134 us -> 124 us (0.925)
  Pallas kernels: 126 us -> 120 us
  other arithmetic: 3.46 us -> 0 us
  local copies, waits for them, and re-layouts: 4.44 us -> 2.69 us
    pallas_call x1, Pallas kernels: 126 us -> 120 us  [moe_call(): pl.pallas_call(functools.partial(moe_kernel, chunks, width), out_shape=ja...]
where the time goes in v2:
time: 124 us; the launch traced here: 123 us
  Pallas kernels  120 us (97%)
  local copies, waits for them, and re-layouts  2.69 us (2%)
    pallas_call x1, Pallas kernels, moe_call(): pl.pallas_call(functools.partial(moe_kernel, chunks, width), out_shape=ja...  120 us
    unnamed x1, local copies, waits for them, and re-layouts  2.69 us

profile of v2, /device:TPU:0, one launch (start us, length us, event | category | flops | bytes accessed | tf_op | source)
XLA Modules:
  0.0 123.1 jit_solution(1391160584854958814)
XLA Ops:
  0.0 120.4 %shard_map.73 = bf16[1,128,6144]{2,1,0:T(8,128)(2,1)} custom-call(s32[1,2,128]{2,1,0:T(2,128)} %bitcast.3, f32[1,2,128]{2,1,0:T(2,128)} %bitcast.4, s32[1,2,128]{2,1,0:T(2,128)} %bitcast.5, bf16[1,128,6144]{2,1,0:T(8,128)(2,1)} %states_ref.1, bf16[1,6144,2048]{2,1,0:T(8,128)(2,1)} %wg_ref.1, bf16[1,6144,2048]{2,1,0:T(8,128)(2,1)} %wu_ref.1, ...), custom_call_target="tpu_custom_call" | custom-call | flops 28991029248 | bytes 75497472 | tf_op jit(solution)/shard_map/pallas_call | solution.py:320
  120.4 2.7 %copy.9 = bf16[1,128,6144]{2,1,0:T(8,128)(2,1)} copy(bf16[1,128,6144]{2,1,0:T(8,128)(2,1)} %shard_map.73) | data formatting | bytes 3145728

commit v3 on v2

--- a/solution.py
+++ b/solution.py
@@ -26,12 +26,12 @@
 
 def moe_kernel(
     chunks, width,
-    ids_ref, gates_ref, keep_ref, states_ref, wg_ref, wu_ref, wd_ref,
+    ids_hbm, gates_hbm, keep_hbm, states_hbm, wg_ref, wu_ref, wd_ref,
     out_ref,
-    tab, spread, wcol,
+    ids_ref, gates_ref, keep_ref, states_ref, tab, spread, wcol,
     rows, other, wg_buf, wu_buf, wd_buf, gate, up, hidden, part,
     sum_y, sum_z, sum_b, sum_a, mixed, landed,
-    send_sem, recv_sem, wg_sem, wu_sem, wd_sem,
+    send_sem, recv_sem, wg_sem, wu_sem, wd_sem, load_sem,
 ):
     section = lax.axis_index("section")
     ep = lax.axis_index("ep")
@@ -109,6 +109,17 @@
             wd_ref.at[0, :, columns], wd_buf.at[slot], wd_sem.at[slot]
         )
 
+    loads = [
+        pltpu.make_async_copy(src, dst, load_sem.at[n])
+        for n, (src, dst) in enumerate((
+            (ids_hbm, ids_ref),
+            (gates_hbm, gates_ref),
+            (keep_hbm, keep_ref),
+            (states_hbm, states_ref),
+        ))
+    ]
+    for load in loads:
+        load.start()
     for k in range(RING):
         for c in in_weights(k):
             c.start()
@@ -116,6 +127,9 @@
     barrier = pltpu.get_barrier_semaphore()
     for dev in (dev_y, dev_z, dev_x, dev_next, dev_prev):
         pl.semaphore_signal(barrier, inc=1, device_id=dev, device_id_type=MESH)
+
+    for load in loads[:3]:
+        load.wait()
 
     tokens = states_ref.shape[1]
     mine = ep // GROUP
@@ -156,10 +170,12 @@
         rows[k, block(A_ME)] = taken[:CAP]
         other[k] = taken[CAP:]
 
-    for k in range(2):
+    loads[3].wait()
+    gather(0)
+    pl.semaphore_wait(barrier, 5)
+    copy(X_CROSS, 0).start()
+    for k in range(1, 3):
         gather(k)
-
-    pl.semaphore_wait(barrier, 5)
 
     for k in range(RING):
         out_weights(k).start()
@@ -177,12 +193,16 @@
     def in_step(i, carry):
         @pl.when(i < chunks)
         def _():
-            for kind in (X_CROSS, X_AY, X_AZ):
-                copy(kind, i).start()
-
-        @pl.when(i + 2 < chunks)
-        def _():
-            gather(i + 2)
+            @pl.when(i + 1 < chunks)
+            def _():
+                copy(X_CROSS, i + 1).start()
+
+            copy(X_AY, i).start()
+            copy(X_AZ, i).start()
+
+        @pl.when(i + 3 < chunks)
+        def _():
+            gather(i + 3)
 
         @pl.when((i >= 2) & (i < chunks + 2))
         def _():
@@ -255,9 +275,9 @@
             for kind in range(X_CROSS, X_FB + 1):
                 copy(kind, i).wait_send()
 
-        @pl.when((i >= 1) & (i < chunks + 1))
-        def _():
-            k = i - 1
+        @pl.when((i >= 2) & (i < chunks + 2))
+        def _():
+            k = i - 2
             copy(R_AQ, k).wait_recv()
             sum_y[k] = (wide(part[k, block(y_then_z_slot(k))]) + wide(landed[1, k])).astype(jnp.bfloat16)
             copy(R_SY, k).start()
@@ -265,9 +285,9 @@
             sum_z[k] = (wide(part[k, block(B_Z)]) + wide(landed[0, k])).astype(jnp.bfloat16)
             copy(R_SZ, k).start()
 
-        @pl.when((i >= 2) & (i < chunks + 2))
-        def _():
-            k = i - 2
+        @pl.when((i >= 3) & (i < chunks + 3))
+        def _():
+            k = i - 3
             copy(R_BY, k).wait_recv()
             copy(R_SZ, k).wait_recv()
             sum_b[k] = (
@@ -278,9 +298,9 @@
             copy(R_SY, k).wait_recv()
             sum_a[k] = wide(part[k, block(A_ME)]) + wide(landed[3, k]) + wide(landed[4, k])
 
-        @pl.when(i >= 4)
-        def _():
-            k = i - 4
+        @pl.when(i >= 5)
+        def _():
+            k = i - 5
             copy(R_CROSS, k).wait_recv()
             unused = jnp.zeros((LANES - 2 * CAP, width), jnp.float32)
             values = jnp.concatenate([sum_a[k], wide(landed[6, k]), unused], axis=0)
@@ -298,7 +318,7 @@
 
         return carry
 
-    lax.fori_loop(0, chunks + 4, out_step, 0)
+    lax.fori_loop(0, chunks + 5, out_step, 0)
 
     def last_step(k, carry):
         copy(R_OUT, k).wait_send()
@@ -315,14 +335,17 @@
     chunks = model // width
     total = 2 * GROUP * CAP
     bf16, f32 = jnp.bfloat16, jnp.float32
-    vmem = pl.BlockSpec(memory_space=pltpu.VMEM)
-    hbm = pl.BlockSpec(memory_space=pl.ANY)
+    hbm = pl.BlockSpec(memory_space=pltpu.HBM)
     return pl.pallas_call(
         functools.partial(moe_kernel, chunks, width),
         out_shape=jax.ShapeDtypeStruct((1, tokens, model), bf16),
-        in_specs=[vmem, vmem, vmem, vmem, hbm, hbm, hbm],
-        out_specs=hbm,
+        in_specs=[hbm] * 7,
+        out_specs=pl.BlockSpec(memory_space=pl.ANY),
         scratch_shapes=[
+            pltpu.VMEM((1, 2, tokens), jnp.int32),
+            pltpu.VMEM((1, 2, tokens), f32),
+            pltpu.VMEM((1, 2, tokens), jnp.int32),
+            pltpu.VMEM((1, tokens, model), bf16),
             pltpu.VMEM((LANES, tokens), bf16),
             pltpu.VMEM((tokens, 2 * LANES), bf16),
             pltpu.VMEM((LANES, 1), f32),
@@ -346,6 +369,7 @@
             pltpu.SemaphoreType.DMA((RING,)),
             pltpu.SemaphoreType.DMA((RING,)),
             pltpu.SemaphoreType.DMA((RING,)),
+            pltpu.SemaphoreType.DMA((4,)),
         ],
         cost_estimate=pl.CostEstimate(
             flops=6 * total * model * units,

time: 124 us -> 124 us (level)
  no operation moved by 1% of the time
where the time goes in v3:
time: 124 us; the launch traced here: 123 us
  Pallas kernels  121 us (98%)
  local copies, waits for them, and re-layouts  2.69 us (2%)
    pallas_call x1, Pallas kernels, moe_call(): pl.pallas_call(functools.partial(moe_kernel, chunks, width), out_shape=ja...  121 us
    unnamed x1, local copies, waits for them, and re-layouts  2.69 us

profile of v3, /device:TPU:0, one launch (start us, length us, event | category | flops | bytes accessed | tf_op | source)
XLA Modules:
  0.0 123.4 jit_solution(9968256274467570806)
XLA Ops:
  0.0 120.7 %shard_map.73 = bf16[1,128,6144]{2,1,0:T(8,128)(2,1)} custom-call(s32[1,2,128]{2,1,0:T(2,128)} %bitcast.3, f32[1,2,128]{2,1,0:T(2,128)} %bitcast.4, s32[1,2,128]{2,1,0:T(2,128)} %bitcast.5, bf16[1,128,6144]{2,1,0:T(8,128)(2,1)} %states_hbm.1, bf16[1,6144,2048]{2,1,0:T(8,128)(2,1)} %wg_ref.1, bf16[1,6144,2048]{2,1,0:T(8,128)(2,1)} %wu_ref.1, ...), custom_call_target="tpu_custom_call" | custom-call | flops 28991029248 | bytes 75497472 | tf_op jit(solution)/shard_map/pallas_call | solution.py:339
  120.7 2.7 %copy.9 = bf16[1,128,6144]{2,1,0:T(8,128)(2,1)} copy(bf16[1,128,6144]{2,1,0:T(8,128)(2,1)} %shard_map.73) | data formatting | bytes 3145728
